TPU v7x, 128 devices: a whole 4x4x4 slice. The times are simulated.
128 devices in a mesh: grp: 4 (over x), smp: 32 (over y, z, core).
Axes of the slice: x: 4, y: 4, z: 4, core: 2. Of those that a mesh axis runs over, the one named last changes fastest.
Arguments:
- hidden: bfloat16 [4, 128, 4, 3584], P('grp', 'smp'), may hold values from -3 to 3
- query: bfloat16 [4, 128, 4, 64, 576], P('grp', 'smp'), may hold values from -40 to 40
- prefill_cache: bfloat16 [4, 8, 2048, 576], P('grp', None, 'smp'), may hold values from -4.5 to 4.5
- suffix_cache: bfloat16 [4, 128, 128, 576], P('grp', 'smp'), may hold values from -4 to 4
- suffix_len: int32 [4, 128], P('grp', 'smp'), may hold values from 1 to 128, 8192 in all within a row
- new_latent: bfloat16 [4, 128, 4, 576], P('grp', 'smp'), may hold values from -4 to 4
- w_uv: bfloat16 [64, 512, 128], P('smp'), may hold values from -0.25 to 0.25
- w_out: bfloat16 [64, 128, 3584], P('smp'), may hold values from -0.25 to 0.25
- ffn_gain: bfloat16 [3584], replicated, may hold values from 0.099609375 to 1.8984375
- expert_ids: int32 [4, 128, 4, 8], P('grp', 'smp'), may hold values from 0 to 127, all different within a row; in each aligned block of 16 rows (0 to 15, 16 to 31, ..., all dimensions but the last counted through in order) at most 2 rows name the same one
- route_weights: float32 [4, 128, 4, 8], P('grp', 'smp'), may hold values from 0.05 to 0.5
- w_gate: bfloat16 [128, 3584, 1024], P(('grp', 'smp')), may hold values from -0.09375 to 0.09375
- w_up: bfloat16 [128, 3584, 1024], P(('grp', 'smp')), may hold values from -0.09375 to 0.09375
- w_down: bfloat16 [128, 1024, 3584], P(('grp', 'smp')), may hold values from -0.1875 to 0.1875
Outputs:
- layer_out: bfloat16 [4, 128, 4, 3584], P('grp', 'smp')
Inputs may be any that keep to these rules, and one draw needn't show every extreme that they name: `expert_ids`: the rows of one device name one expert at most 2 times; every expert is named by some row.
All inputs are finite; a program needn't handle non-finite values. No bound on the sum of `suffix_len` on one device may be relied on, other than what follows from the above.
Results may differ from a plain program's by a relative error of at most 0.024.
Values may be sent and summed in bfloat16 or wider, within the bound.
No kernel may reach another device: no remote copies, remote signals or barrier semaphores. Data moves between devices by JAX's collectives and lax.ppermute only.
A program may use at most 128 MiB of HBM per device.

v0:
```python
import jax
import jax.numpy as jnp
from jax import lax
from jax.experimental import pallas as pl
from jax.experimental.pallas import tpu as pltpu
from jax.sharding import PartitionSpec as P

D = 3584
HEADS = 64
LAT = 512
ROPE = 64
NOPE = 128
FF = 1024
TOP = 8
STEPS = 4
SUF = 128
TOK = 16
EXPERTS = 128
QTR = 4
WIDE = D // QTR
SCALE = (NOPE + ROPE) ** (-0.5)
F32 = jnp.float32
BF16 = jnp.bfloat16
MIB = 1024 * 1024


def dot(a, b):
    return jnp.dot(a, b, preferred_element_type=F32)


def dot_t(a, b):
    return lax.dot_general(a, b, (((1,), (1,)), ((), ())), preferred_element_type=F32)


def iota(shape, dim):
    return lax.broadcasted_iota(jnp.int32, shape, dim)


def params(mib):
    return pltpu.CompilerParams(vmem_limit_bytes=mib * MIB)


def attend_body(len_ref, q_ref, ka_ref, kb_ref, own_ref, fresh_ref, out_ref, held):
    samples, rows, _ = q_ref.shape
    step = iota((rows, STEPS), 0) // HEADS
    causal = iota((rows, STEPS), 1) <= step
    slot = iota((rows, SUF), 1)

    def score(s):
        q = q_ref[s]
        own = jnp.where(slot < len_ref[0, s], dot(q, own_ref[s]), -jnp.inf)
        fresh = jnp.where(causal, dot_t(q, fresh_ref[s]), -jnp.inf)
        return [dot_t(q, ka_ref[...]), dot_t(q, kb_ref[...]), own, fresh]

    def settle(s, scores):
        top = jnp.max(scores[0], -1, keepdims=True)
        for sc in scores[1:]:
            top = jnp.maximum(top, jnp.max(sc, -1, keepdims=True))
        total = jnp.zeros((rows, 1), F32)
        acc = jnp.zeros((rows, LAT), F32)
        for i, sc in enumerate(scores):
            p = jnp.exp((sc - top) * SCALE)
            total = total + jnp.sum(p, -1, keepdims=True)
            p = p.astype(BF16)
            if i == 2:
                acc = acc + dot_t(p, own_ref[s, :LAT, :])
            else:
                acc = acc + dot(p, (ka_ref, kb_ref, None, fresh_ref.at[s])[i][:, :LAT])
        ctx = (acc / total).astype(BF16)
        for t in range(STEPS):
            held[s * STEPS + t] = ctx[t * HEADS : (t + 1) * HEADS]

    ahead = score(0)
    for s in range(samples):
        now = ahead
        if s + 1 < samples:
            ahead = score(s + 1)
        settle(s, now)
    n = TOK * 16
    perm = (iota((n, n), 1) == (iota((n, n), 0) % TOK) * 16 + iota((n, n), 0) // TOK).astype(BF16)
    for b in range(HEADS // 16):
        part = held[:, b * 16 : (b + 1) * 16, :].reshape(n, LAT)
        out_ref[b * 16 : (b + 1) * 16] = dot(perm, part).astype(BF16).reshape(16, TOK, LAT)


def attend(lens, q, ka, kb, own, fresh):
    samples, rows, width = q.shape
    half = ka.shape[0]
    vmem = pl.BlockSpec(memory_space=pltpu.VMEM)
    return pl.pallas_call(
        attend_body,
        in_specs=[pl.BlockSpec(memory_space=pltpu.SMEM)] + [vmem] * 5,
        out_specs=vmem,
        out_shape=jax.ShapeDtypeStruct((HEADS, TOK, LAT), BF16),
        scratch_shapes=[pltpu.VMEM((TOK, HEADS, LAT), BF16)],
        compiler_params=params(32),
        cost_estimate=pl.CostEstimate(
            flops=2 * samples * rows * (2 * half + SUF) * (width + LAT),
            bytes_accessed=8 * 1024 * 1024,
            transcendentals=samples * rows * (2 * half + SUF),
        ),
        name="attend",
    )(lens, q, ka, kb, own, fresh)


def project_body(core_ref, x_ref, uva_ref, uvb_ref, oa_ref, ob_ref, out_ref):
    chips, _, tok, _ = x_ref.shape
    rows = chips * tok
    core = core_ref[0]
    sides = []
    for side, uv in enumerate((uva_ref, uvb_ref)):
        first = 2 * core if side == 0 else 2 * (1 - core)
        cols = [dot(x_ref[:, pl.ds(first + h, 1)].reshape(rows, LAT), uv[h]).astype(BF16) for h in range(2)]
        sides.append(jnp.concatenate(cols, axis=1))
    both = jnp.concatenate(sides, axis=1)
    for c in range(D // 512):
        span = slice(c * 512, (c + 1) * 512)
        w = jnp.concatenate([o[:, :, span].reshape(2 * NOPE, 512) for o in (oa_ref, ob_ref)], axis=0)
        out_ref[:, :, span] = dot(both, w).astype(BF16).reshape(chips, tok, 512)


def project(core, x, uva, uvb, oa, ob):
    chips, _, tok, _ = x.shape
    vmem = pl.BlockSpec(memory_space=pltpu.VMEM)
    return pl.pallas_call(
        project_body,
        in_specs=[pl.BlockSpec(memory_space=pltpu.SMEM)] + [vmem] * 5,
        out_specs=vmem,
        out_shape=jax.ShapeDtypeStruct((chips, tok, D), BF16),
        compiler_params=params(20),
        cost_estimate=pl.CostEstimate(flops=1100000000, bytes_accessed=7 * 1024 * 1024, transcendentals=0),
        name="project",
    )(core, x, uva, uvb, oa, ob)


def route_body(ids_ref, w_ref, send_ref, mix_ref):
    lines = EXPERTS * 2 * QTR
    ids = ids_ref[...]
    w = w_ref[...]
    lane = iota((TOK, EXPERTS), 1)
    named = jnp.zeros((TOK, EXPERTS), F32)
    weight = jnp.zeros((TOK, EXPERTS), F32)
    for k in range(TOP):
        hit = ids[:, k : k + 1] == lane
        named = named + jnp.where(hit, 1.0, 0.0)
        weight = weight + jnp.where(hit, w[:, k : k + 1], 0.0)
    below = (iota((TOK, TOK), 1) < iota((TOK, TOK), 0)).astype(BF16)
    earlier = dot(below, named.astype(BF16))
    spread = (iota((EXPERTS, lines), 1) // (2 * QTR) == iota((EXPERTS, lines), 0)).astype(BF16)
    high = weight.astype(BF16)
    low = (weight - high.astype(F32)).astype(BF16)
    stack = jnp.concatenate([named.astype(BF16), earlier.astype(BF16), high, low], axis=0)
    wide = dot(stack, spread)
    named, earlier, high, low = (wide[i * TOK : (i + 1) * TOK] for i in range(4))
    col = iota((TOK, lines), 1)
    slot = (col % (2 * QTR)) // QTR
    chosen = jnp.logical_and(named > 0.5, jnp.abs(earlier - slot.astype(F32)) < 0.5)
    sel = []
    for q in range(QTR):
        here = jnp.logical_and(chosen, col % QTR == q)
        sel.append(jnp.where(here, 1.0, 0.0))
        mix_ref[q * TOK : (q + 1) * TOK, :] = jnp.where(here, high, 0.0).astype(BF16)
        mix_ref[(QTR + q) * TOK : (QTR + q + 1) * TOK, :] = jnp.where(here, low, 0.0).astype(BF16)
    send_ref[...] = jnp.concatenate(sel, axis=0).T.astype(BF16)


def route(ids, w):
    lines = EXPERTS * 2 * QTR
    return pl.pallas_call(
        route_body,
        out_shape=(
            jax.ShapeDtypeStruct((lines, QTR * TOK), BF16),
            jax.ShapeDtypeStruct((2 * QTR * TOK, lines), BF16),
        ),
        compiler_params=params(8),
        name="route",
    )(ids, w)


def dispatch_body(parts_ref, hid_ref, gain_ref, send_ref, res_ref, out_ref):
    total = parts_ref[0].astype(F32)
    for i in range(1, parts_ref.shape[0]):
        total = total + parts_ref[i].astype(F32)
    residual = hid_ref[...].reshape(TOK, D).astype(F32) + total
    res_ref[...] = residual
    mean = jnp.mean(residual * residual, axis=-1, keepdims=True)
    norm = (residual * lax.rsqrt(mean + 1e-06) * gain_ref[...].astype(F32)).astype(BF16)
    tall = jnp.concatenate([norm[:, q * WIDE : (q + 1) * WIDE] for q in range(QTR)], axis=0)
    out_ref[...] = dot(send_ref[...], tall).astype(BF16)


def dispatch(parts, hid, gain, send):
    return pl.pallas_call(
        dispatch_body,
        out_shape=(
            jax.ShapeDtypeStruct((TOK, D), F32),
            jax.ShapeDtypeStruct((send.shape[0], WIDE), BF16),
        ),
        compiler_params=params(14),
        name="dispatch",
    )(parts, hid, gain, send)


CHUNK = 512
PIECES = D // CHUNK
FLYING = 5


def expert_body(x, wg, wu, wd_hbm, out_ref, xs, wd, mid, res, sems):
    lines = x.shape[0]
    rows = lines // QTR
    group = rows // 4
    loads = []
    for c in range(PIECES):
        span = pl.ds(c * CHUNK, CHUNK)
        loads.append(pltpu.make_async_copy(wd_hbm.at[0, :, span], wd.at[:, span], sems.at[c]))
    for i in range(FLYING):
        loads[i].start()

    def take(i):
        loads[i].wait()
        if i + FLYING < len(loads):
            loads[i + FLYING].start()

    n = lines // 4
    out_row, in_row = iota((n, n), 0), iota((n, n), 1)
    perm = (in_row == (out_row % group) * QTR + out_row // group).astype(BF16)
    unperm = (out_row == (in_row % group) * QTR + in_row // group).astype(BF16)
    for i in range(4):
        part = dot(perm, x[i * n : (i + 1) * n, :]).astype(BF16)
        for q in range(QTR):
            xs[i * group : (i + 1) * group, q * WIDE : (q + 1) * WIDE] = part[q * group : (q + 1) * group]
    gate = dot(xs[...], wg[0])
    gate = gate / (1.0 + jnp.exp(-gate))
    up = dot(xs[...], wu[0])
    mid[...] = (gate * up).astype(BF16)
    for c in range(PIECES):
        take(c)
        span = slice(c * CHUNK, (c + 1) * CHUNK)
        res[:, span] = dot(mid[...], wd[:, span]).astype(BF16)
    for i in range(4):
        part = [res[i * group : (i + 1) * group, q * WIDE : (q + 1) * WIDE] for q in range(QTR)]
        out_ref[i * n : (i + 1) * n, :] = dot(unperm, jnp.concatenate(part, axis=0)).astype(BF16)


def expert(x, wg, wu, wd):
    lines = x.shape[0]
    rows = lines // QTR
    vmem = pl.BlockSpec(memory_space=pltpu.VMEM)
    hbm = pl.BlockSpec(memory_space=pl.ANY)
    return pl.pallas_call(
        expert_body,
        in_specs=[vmem, vmem, vmem, hbm],
        out_specs=vmem,
        out_shape=jax.ShapeDtypeStruct(x.shape, BF16),
        scratch_shapes=[
            pltpu.VMEM((rows, D), BF16),
            pltpu.VMEM((FF, D), BF16),
            pltpu.VMEM((rows, FF), BF16),
            pltpu.VMEM((rows, D), BF16),
            pltpu.SemaphoreType.DMA((PIECES,)),
        ],
        compiler_params=params(36),
        cost_estimate=pl.CostEstimate(
            flops=6 * rows * D * FF, bytes_accessed=26 * 1024 * 1024, transcendentals=rows * FF
        ),
        name="expert",
    )(x, wg, wu, wd)


def combine_body(mix_ref, back_ref, res_ref, out_ref):
    both = dot(mix_ref[...], back_ref[...])
    n = QTR * TOK
    y = both[:n] + both[n:]
    for q in range(QTR):
        span = slice(q * WIDE, (q + 1) * WIDE)
        z = (res_ref[:, span] + y[q * TOK : (q + 1) * TOK]).astype(BF16)
        for s in range(TOK // STEPS):
            out_ref[0, s, :, span] = z[s * STEPS : (s + 1) * STEPS]


def combine(mix, back, res):
    return pl.pallas_call(
        combine_body,
        out_shape=jax.ShapeDtypeStruct((1, TOK // STEPS, STEPS, D), BF16),
        compiler_params=params(10),
        name="combine",
    )(mix, back, res)


def on_device(
    hidden,
    query,
    prefill_cache,
    suffix_cache,
    suffix_len,
    new_latent,
    w_uv,
    w_out,
    ffn_gain,
    expert_ids,
    route_weights,
    w_gate,
    w_up,
    w_down,
):
    samples = query.shape[1]
    n_smp = lax.axis_size("smp")
    chips = n_smp // 2
    prompts, span, width = prefill_cache.shape[1:]
    core = lax.axis_index("smp") % 2
    pair = [(i, i ^ 1) for i in range(n_smp)]
    same_core = [[2 * k + c for k in range(chips)] for c in range(2)]

    shared = n_smp // prompts // 2
    slab = prefill_cache[0].reshape(prompts, 1, 2, span // 2, width)
    outgoing = jnp.broadcast_to(slab, (prompts, shared, 2, span // 2, width)).reshape(n_smp, span // 2, width)
    half_a = lax.all_to_all(outgoing, "smp", 0, 0, tiled=True)

    half_a, ids, weights, gain = lax.optimization_barrier((half_a, expert_ids, route_weights, ffn_gain))
    half_b = lax.ppermute(half_a, "smp", pair)
    send, mix = route(ids.reshape(TOK, TOP), weights.reshape(TOK, TOP))
    gain = gain.reshape(1, D)
    core = core.reshape(1)
    half_b, send, mix, gain, core, w_uv, w_out = lax.optimization_barrier(
        (half_b, send, mix, gain, core, w_uv, w_out)
    )
    uv_b = lax.ppermute(w_uv, "smp", pair)
    out_b = lax.ppermute(w_out, "smp", pair)
    half_a = half_a.reshape(-1, width)
    half_b = half_b.reshape(-1, width)
    own = jnp.swapaxes(suffix_cache[0], 1, 2)
    context = attend(
        suffix_len, query.reshape(samples, STEPS * HEADS, width), half_a, half_b, own, new_latent[0]
    )
    context, uv_b, out_b = lax.optimization_barrier((context, uv_b, out_b))
    by_chip = context.reshape(chips, HEADS // chips, TOK, LAT)
    by_heads = lax.all_to_all(by_chip, "smp", 0, 0, tiled=True, axis_index_groups=same_core)
    shares = project(core, by_heads, w_uv, uv_b, w_out, out_b)
    parts = lax.all_to_all(shares, "smp", 0, 0, tiled=True, axis_index_groups=same_core)
    residual, rows = dispatch(parts, hidden[0], gain, send)

    rows = rows.reshape(EXPERTS, 2 * QTR, WIDE)
    arrived = lax.all_to_all(rows, ("grp", "smp"), 0, 0, tiled=True)
    answered = expert(arrived.reshape(-1, WIDE), w_gate, w_up, w_down)
    answered = answered.reshape(EXPERTS, 2 * QTR, WIDE)
    returned = lax.all_to_all(answered, ("grp", "smp"), 0, 0, tiled=True)
    return combine(mix, returned.reshape(-1, WIDE), residual)


def solution(mesh):
    placed = (
        P("grp", "smp", None, None),
        P("grp", "smp", None, None, None),
        P("grp", None, "smp", None),
        P("grp", "smp", None, None),
        P("grp", "smp"),
        P("grp", "smp", None, None),
        P("smp", None, None),
        P("smp", None, None),
        P(),
        P("grp", "smp", None, None),
        P("grp", "smp", None, None),
        P(("grp", "smp"), None, None),
        P(("grp", "smp"), None, None),
        P(("grp", "smp"), None, None),
    )
    return jax.shard_map(
        on_device,
        mesh=mesh,
        in_specs=placed,
        out_specs=P("grp", "smp", None, None),
        check_vma=False,
    )
```

profile of v0, /device:TPU:1, one launch (start us, length us, event | category | flops | bytes accessed | tf_op | source)
XLA Modules:
  0.0 173.5 jit_solution(4728039580043804477)
XLA Ops:
  0.0 0.0 copy-start.9
  0.0 0.0 copy-start.3
  0.0 0.0 copy-start.4
  0.0 1.3 broadcast_in_dim.8
  1.3 0.0 copy-start
  1.3 0.0 copy-start.1
  1.3 0.0 copy-start.7
  1.3 0.0 copy-start.8
  1.4 29.8 %all_to_all.25 = bf16[32,32,576]{2,1,0:T(8,128)(2,1)S(1)} all-to-all(bf16[32,32,576]{2,1,0:T(8,128)(2,1)S(1)} %bitcast.34), channel_id=1, replica_groups=mesh['grp'=4,'smp'=32] {'smp'}, dimensions={0} | all-to-all | bytes 2359296 | tf_op jit(solution)/shard_map/all_to_all | solution.py:318
  31.1 0.2 collective-permute-start
  31.3 0.0 copy-done.9
  31.3 0.0 copy-done.3
  31.3 0.0 copy-done.4
  31.3 0.5 route.1
  31.8 2.4 %collective-permute-done = bf16[32,32,576]{2,1,0:T(8,128)(2,1)} collective-permute-done((bf16[32,32,576]{2,1,0:T(8,128)(2,1)S(1)}, bf16[32,32,576]{2,1,0:T(8,128)(2,1)}, u32[]{:S(2)}, u32[]{:S(2)}) %collective-permute-start) | collective-permute-done | bytes 1179680 | tf_op jit(solution)/shard_map/ppermute | solution.py:321
  34.3 0.0 copy-done
  34.3 0.2 collective-permute-start.2
  34.5 0.0 copy-done.1
  34.5 0.3 collective-permute-start.1
  34.8 0.0 copy-done.7
  34.8 0.0 copy-done.8
  34.8 0.0 copy-start.5
  34.8 1.3 copy-done.5
  36.1 0.0 copy-start.6
  36.1 1.1 copy-done.6
  37.2 0.0 slice-start.2
  37.2 9.3 %attend.1 = bf16[64,16,512]{2,1,0:T(8,128)(2,1)S(1)} custom-call(s32[1,4]{1,0:T(1,128)S(1)} %copy-done.8, bf16[4,256,576]{2,1,0:T(8,128)(2,1)S(1)} %bitcast.31, bf16[1024,576]{1,0:T(8,128)(2,1)S(1)} %bitcast.26, bf16[1024,576]{1,0:T(8,128)(2,1)} %bitcast.7.kb_ref, bf16[4,576,128]{2,1,0:T(8,128)(2,1)S(1)} %bitcast.32, bf16[4,4,576]{2,1,0:T(4,128)(2,1)S(1)} %bitcast.33), custom_call_target="tpu_custom_call" | custom-call | flops 4848615424 | bytes 8388608 | tf_op jit(solution)/shard_map/attend/pallas_call | solution.py:90
  46.5 0.0 collective-permute-done.1.uvb_ref
  46.5 0.0 collective-permute-done.2.ob_ref
  46.5 0.0 slice-start.3
  46.5 19.0 %all_to_all.26.x_ref = bf16[16,4,16,512]{3,2,1,0:T(8,128)(2,1)S(1)} all-to-all(bf16[16,4,16,512]{3,2,1,0:T(8,128)(2,1)S(1)} %bitcast.27), channel_id=1, replica_groups={{0,2,4,6,8,10,12,14,16,18,20,22,24,26,28,30},{1,3,5,7,9,11,13,15,17,19,..., dimensions={0} | all-to-all | bytes 2097152 | tf_op jit(solution)/shard_map/all_to_all | solution.py:338
  65.5 0.0 slice-start
  65.5 1.4 project.1
  66.9 0.0 copy-start.2
  66.9 0.0 slice-start.1
  67.0 26.8 %all_to_all.27.parts_ref = bf16[16,16,3584]{2,1,0:T(8,128)(2,1)S(1)} all-to-all(bf16[16,16,3584]{2,1,0:T(8,128)(2,1)S(1)} %project.1), channel_id=1, replica_groups={{0,2,4,6,8,10,12,14,16,18,20,22,24,26,28,30},{1,3,5,7,9,11,13,15,17,19,..., dimensions={0} | all-to-all | bytes 3670016 | tf_op jit(solution)/shard_map/all_to_all | solution.py:340
  93.7 0.0 copy-done.2
  93.7 1.1 dispatch.1
  94.8 36.4 %all_to_all.28 = bf16[128,8,896]{2,1,0:T(8,128)(2,1)S(1)} all-to-all(bf16[128,8,896]{2,1,0:T(8,128)(2,1)S(1)} %bitcast.25), channel_id=1, replica_groups=mesh['grp'=4,'smp'=32] {'grp','smp'}, dimensions={0} | all-to-all | bytes 3670016 | tf_op jit(solution)/shard_map/all_to_all | solution.py:344
  131.2 0.0 slice-done.2
  131.2 0.0 slice-done.3
  131.2 0.0 slice-done
  131.2 0.0 slice-done.1
  131.3 9.3 %expert.1 = bf16[1024,896]{1,0:T(8,128)(2,1)S(1)} custom-call(bf16[1024,896]{1,0:T(8,128)(2,1)S(1)} %bitcast.18, bf16[1,3584,1024]{2,1,0:T(8,128)(2,1)S(1)} %bitcast.22, bf16[1,3584,1024]{2,1,0:T(8,128)(2,1)S(1)} %bitcast.24, bf16[1,1024,3584]{2,1,0:T(8,128)(2,1)} %wd_hbm.1), custom_call_target="tpu_custom_call" | custom-call | flops 5637144576 | bytes 27262976 | tf_op jit(solution)/shard_map/expert/pallas_call | solution.py:251
  140.5 31.8 %all_to_all.29 = bf16[128,8,896]{2,1,0:T(8,128)(2,1)S(1)} all-to-all(bf16[128,8,896]{2,1,0:T(8,128)(2,1)S(1)} %bitcast.19), channel_id=1, replica_groups=mesh['grp'=4,'smp'=32] {'grp','smp'}, dimensions={0} | all-to-all | bytes 3670016 | tf_op jit(solution)/shard_map/all_to_all | solution.py:347
  172.4 1.1 combine.1
  (3 shorter events, 0.0 us)
Async XLA Ops:
  0.0 31.3 %copy-start.9 = (bf16[3584]{0:T(1024)(128)(2,1)S(1)}, bf16[3584]{0:T(1024)(128)(2,1)}, u32[]{:S(2)}) copy-start(bf16[3584]{0:T(1024)(128)(2,1)} %param.22) | copy-start | bytes 21508
  0.0 31.3 %copy-start.3 = (s32[1,4,4,8]{3,2,1,0:T(4,128)S(1)}, s32[1,4,4,8]{3,2,1,0:T(4,128)}, u32[]{:S(2)}) copy-start(s32[1,4,4,8]{3,2,1,0:T(4,128)} %param.23) | copy-start | bytes 1540
  0.0 31.3 %copy-start.4 = (f32[1,4,4,8]{3,2,1,0:T(4,128)S(1)}, f32[1,4,4,8]{3,2,1,0:T(4,128)}, u32[]{:S(2)}) copy-start(f32[1,4,4,8]{3,2,1,0:T(4,128)} %param.24) | copy-start | bytes 1540
  1.3 33.0 %copy-start = (bf16[2,128,3584]{2,1,0:T(8,128)(2,1)S(1)}, bf16[2,128,3584]{2,1,0:T(8,128)(2,1)}, u32[]{:S(2)}) copy-start(bf16[2,128,3584]{2,1,0:T(8,128)(2,1)} %oa_ref) | copy-start | bytes 5505028
  1.3 33.2 %copy-start.1 = (bf16[2,512,128]{2,1,0:T(8,128)(2,1)S(1)}, bf16[2,512,128]{2,1,0:T(8,128)(2,1)}, u32[]{:S(2)}) copy-start(bf16[2,512,128]{2,1,0:T(8,128)(2,1)} %uva_ref) | copy-start | bytes 786436
  1.3 33.5 %copy-start.7 = (bf16[1,4,4,576]{3,2,1,0:T(4,128)(2,1)S(1)}, bf16[1,4,4,576]{3,2,1,0:T(4,128)(2,1)}, u32[]{:S(2)}) copy-start(bf16[1,4,4,576]{3,2,1,0:T(4,128)(2,1)} %param.19) | copy-start | bytes 55300
  1.3 33.5 %copy-start.8 = (s32[1,4]{1,0:T(1,128)S(1)}, s32[1,4]{1,0:T(1,128)}, u32[]{:S(2)}) copy-start(s32[1,4]{1,0:T(1,128)} %len_ref.1) | copy-start | bytes 52
  31.1 3.2 %collective-permute-start = (bf16[32,32,576]{2,1,0:T(8,128)(2,1)S(1)}, bf16[32,32,576]{2,1,0:T(8,128)(2,1)}, u32[]{:S(2)}, u32[]{:S(2)}) collective-permute-start(bf16[32,32,576]{2,1,0:T(8,128)(2,1)S(1)} %all_to_all.25), channel_id=1, source_target_pairs={{0,1},{1,0},{2,3},{3,2},{4,5},{5,4},{6,7},{7,6},{8,9},{9,8},{10,11... | collective-permute-start | bytes 3538952 | tf_op jit(solution)/shard_map/ppermute | solution.py:321
  34.3 12.2 %collective-permute-start.2 = (bf16[2,128,3584]{2,1,0:T(8,128)(2,1)S(1)}, bf16[2,128,3584]{2,1,0:T(8,128)(2,1)S(1)}, u32[]{:S(2)}, u32[]{:S(2)}) collective-permute-start(bf16[2,128,3584]{2,1,0:T(8,128)(2,1)S(1)} %copy-done), channel_id=1, source_target_pairs={{0,1},{1,0},{2,3},{3,2},{4,5},{5,4},{6,7},{7,6},{8,9},{9,8},{10,11... | collective-permute-start | bytes 5505032 | tf_op jit(solution)/shard_map/ppermute | solution.py:329
  34.5 12.0 %collective-permute-start.1 = (bf16[2,512,128]{2,1,0:T(8,128)(2,1)S(1)}, bf16[2,512,128]{2,1,0:T(8,128)(2,1)S(1)}, u32[]{:S(2)}, u32[]{:S(2)}) collective-permute-start(bf16[2,512,128]{2,1,0:T(8,128)(2,1)S(1)} %copy-done.1), channel_id=1, source_target_pairs={{0,1},{1,0},{2,3},{3,2},{4,5},{5,4},{6,7},{7,6},{8,9},{9,8},{10,11... | collective-permute-start | bytes 786440 | tf_op jit(solution)/shard_map/ppermute | solution.py:328
  34.8 1.3 copy-start.5
  36.1 1.1 copy-start.6
  37.2 94.0 %slice-start.2 = ((s8[7340032]{0:T(1024)(128)(4,1)}), s8[4194304]{0:T(1024)(128)(4,1)S(1)}, s32[]{:S(2)}) async-start(s8[7340032]{0:T(1024)(128)(4,1)} %bitcast.23), calls=%async_computation.7 | async-start | bytes 8388608
  46.5 84.7 %slice-start.3 = ((s8[7340032]{0:T(1024)(128)(4,1)}), s8[3145728]{0:T(1024)(128)(4,1)S(1)}, s32[]{:S(2)}) async-start(s8[7340032]{0:T(1024)(128)(4,1)} %bitcast.23), calls=%async_computation.8 | async-start | bytes 6291456
  65.5 65.7 %slice-start = ((s8[7340032]{0:T(1024)(128)(4,1)}), s8[4194304]{0:T(1024)(128)(4,1)S(1)}, s32[]{:S(2)}) async-start(s8[7340032]{0:T(1024)(128)(4,1)} %bitcast.21), calls=%async_computation.5 | async-start | bytes 8388608
  66.9 26.8 %copy-start.2 = (bf16[1,4,4,3584]{3,2,1,0:T(4,128)(2,1)S(1)}, bf16[1,4,4,3584]{3,2,1,0:T(4,128)(2,1)}, u32[]{:S(2)}) copy-start(bf16[1,4,4,3584]{3,2,1,0:T(4,128)(2,1)} %param.14) | copy-start | bytes 344068
  66.9 64.3 %slice-start.1 = ((s8[7340032]{0:T(1024)(128)(4,1)}), s8[3145728]{0:T(1024)(128)(4,1)S(1)}, s32[]{:S(2)}) async-start(s8[7340032]{0:T(1024)(128)(4,1)} %bitcast.21), calls=%async_computation.6 | async-start | bytes 6291456
where the time goes:
time: 174 us; the launch traced here: 173 us
  blocking collectives  144 us (83%)
  Pallas kernels  22.6 us (13%)
  local copies, waits for them, and re-layouts  3.75 us (2%)
  waiting for transfers between devices  2.44 us (1%)
    all_to_all x1, blocking collectives, on_device(): arrived = lax.all_to_all(rows, ('grp', 'smp'), 0, 0, tiled=True)  36.4 us
    all_to_all x1, blocking collectives, on_device(): returned = lax.all_to_all(answered, ('grp', 'smp'), 0, 0, tiled=True)  31.8 us
    all_to_all x1, blocking collectives, on_device(): half_a = lax.all_to_all(outgoing, 'smp', 0, 0, tiled=True)  29.8 us
    all_to_all x1, blocking collectives, on_device(): lax.all_to_all(shares, 'smp', 0, 0, tiled=True, axis_index_groups=same_core)  26.8 us
    all_to_all x1, blocking collectives, on_device(): lax.all_to_all(by_chip, 'smp', 0, 0, tiled=True, axis_index_groups=same_c...  19 us
    pallas_call x1, Pallas kernels, attend(): pl.pallas_call(attend_body, in_specs=[pl.BlockSpec(memory_space=pltpu.SME...  9.3 us
    pallas_call x1, Pallas kernels, expert(): pl.pallas_call(expert_body, in_specs=[vmem, vmem, vmem, hbm], out_specs=v...  9.28 us
  transfers between devices with their start and end apart: 3, of which 1 were waited for; matrix products, arithmetic and copies ran while one was open for 0% of the time, Pallas kernels for 6%

commit v1 on v0

--- a/solution.py
+++ b/solution.py
@@ -40,19 +40,93 @@
     return pltpu.CompilerParams(vmem_limit_bytes=mib * MIB)
 
 
-def attend_body(len_ref, q_ref, ka_ref, kb_ref, own_ref, fresh_ref, out_ref, held):
+SPAN = 32
+LINES = SPAN * 4 + SPAN // 2
+HALF = SPAN // 2
+
+
+def pack_body(slab_ref, out_ref):
+    prompts, span, _ = slab_ref.shape
+    for p in range(prompts):
+        for c in range(span // SPAN):
+            x = slab_ref[p, c * SPAN : (c + 1) * SPAN, :]
+            tiles = [x[:, i * 128 : (i + 1) * 128] for i in range(LAT // 128)]
+            tiles.append(jnp.concatenate([x[:HALF, LAT:], x[HALF:, LAT:]], axis=1))
+            block = jnp.concatenate(tiles, axis=0)
+            for j in range(out_ref.shape[1]):
+                out_ref[p, j, c] = block
+
+
+def pack(slab, shared):
+    prompts, span, _ = slab.shape
+    vmem = pl.BlockSpec(memory_space=pltpu.VMEM)
+    return pl.pallas_call(
+        pack_body,
+        in_specs=[vmem],
+        out_specs=vmem,
+        out_shape=jax.ShapeDtypeStruct((prompts, shared, span // SPAN, LINES, 128), BF16),
+        compiler_params=params(8),
+        name="pack",
+    )(slab)
+
+
+def latents(ref, g):
+    tiles = [ref[:, i * SPAN + g * HALF : i * SPAN + (g + 1) * HALF, :] for i in range(LAT // 128)]
+    return jnp.concatenate([t.reshape(-1, 128) for t in tiles], axis=1)
+
+
+def keys(ref, g):
+    return jnp.concatenate([latents(ref, g), ref[:, 4 * SPAN :, :].reshape(-1, 128)], axis=1)
+
+
+def packed_scores(q, ref):
+    gap = jnp.zeros((q.shape[0], ROPE), BF16)
+    first = jnp.concatenate([q, gap], axis=1)
+    second = jnp.concatenate([q[:, :LAT], gap, q[:, LAT:]], axis=1)
+    return jnp.concatenate([dot_t(first, keys(ref, 0)), dot_t(second, keys(ref, 1))], axis=1)
+
+
+def values(ref):
+    return jnp.concatenate([latents(ref, 0), latents(ref, 1)], axis=0)
+
+
+def score_body(len_ref, q_ref, ka_ref, own_ref, fresh_ref, sa_ref, so_ref, sf_ref):
     samples, rows, _ = q_ref.shape
-    step = iota((rows, STEPS), 0) // HEADS
-    causal = iota((rows, STEPS), 1) <= step
+    causal = iota((rows, STEPS), 1) <= iota((rows, STEPS), 0) // HEADS
     slot = iota((rows, SUF), 1)
-
-    def score(s):
+    for s in range(samples):
         q = q_ref[s]
-        own = jnp.where(slot < len_ref[0, s], dot(q, own_ref[s]), -jnp.inf)
-        fresh = jnp.where(causal, dot_t(q, fresh_ref[s]), -jnp.inf)
-        return [dot_t(q, ka_ref[...]), dot_t(q, kb_ref[...]), own, fresh]
-
-    def settle(s, scores):
+        sa_ref[s] = packed_scores(q, ka_ref)
+        sf_ref[s] = jnp.where(causal, dot_t(q, fresh_ref[s]), -jnp.inf)
+        so_ref[s] = jnp.where(slot < len_ref[0, s], dot(q, own_ref[s]), -jnp.inf)
+
+
+def score(lens, q, ka, own, fresh):
+    samples, rows, width = q.shape
+    half = ka.shape[0] * SPAN
+    vmem = pl.BlockSpec(memory_space=pltpu.VMEM)
+    return pl.pallas_call(
+        score_body,
+        in_specs=[pl.BlockSpec(memory_space=pltpu.SMEM)] + [vmem] * 4,
+        out_specs=[vmem] * 3,
+        out_shape=(
+            jax.ShapeDtypeStruct((samples, rows, half), F32),
+            jax.ShapeDtypeStruct((samples, rows, SUF), F32),
+            jax.ShapeDtypeStruct((samples, rows, STEPS), F32),
+        ),
+        compiler_params=params(18),
+        cost_estimate=pl.CostEstimate(
+            flops=2 * samples * rows * (half + SUF) * width, bytes_accessed=2 * 1024 * 1024, transcendentals=0
+        ),
+        name="score",
+    )(lens, q, ka, own, fresh)
+
+
+def attend_body(q_ref, own_ref, sa_ref, so_ref, sf_ref, ka_ref, kb_ref, fresh_ref, out_ref, held):
+    samples, rows, _ = q_ref.shape
+
+    def settle(s, ahead):
+        scores = [sa_ref[s], ahead, so_ref[s], sf_ref[s]]
         top = jnp.max(scores[0], -1, keepdims=True)
         for sc in scores[1:]:
             top = jnp.maximum(top, jnp.max(sc, -1, keepdims=True))
@@ -64,17 +138,19 @@
             p = p.astype(BF16)
             if i == 2:
                 acc = acc + dot_t(p, own_ref[s, :LAT, :])
+            elif i == 3:
+                acc = acc + dot(p, fresh_ref[s, :, :LAT])
             else:
-                acc = acc + dot(p, (ka_ref, kb_ref, None, fresh_ref.at[s])[i][:, :LAT])
+                acc = acc + dot(p, values((ka_ref, kb_ref)[i]))
         ctx = (acc / total).astype(BF16)
         for t in range(STEPS):
             held[s * STEPS + t] = ctx[t * HEADS : (t + 1) * HEADS]
 
-    ahead = score(0)
+    ahead = packed_scores(q_ref[0], kb_ref)
     for s in range(samples):
         now = ahead
         if s + 1 < samples:
-            ahead = score(s + 1)
+            ahead = packed_scores(q_ref[s + 1], kb_ref)
         settle(s, now)
     n = TOK * 16
     perm = (iota((n, n), 1) == (iota((n, n), 0) % TOK) * 16 + iota((n, n), 0) // TOK).astype(BF16)
@@ -83,24 +159,24 @@
         out_ref[b * 16 : (b + 1) * 16] = dot(perm, part).astype(BF16).reshape(16, TOK, LAT)
 
 
-def attend(lens, q, ka, kb, own, fresh):
+def attend(q, own, scored, ka, kb, fresh):
     samples, rows, width = q.shape
-    half = ka.shape[0]
+    half = ka.shape[0] * SPAN
     vmem = pl.BlockSpec(memory_space=pltpu.VMEM)
     return pl.pallas_call(
         attend_body,
-        in_specs=[pl.BlockSpec(memory_space=pltpu.SMEM)] + [vmem] * 5,
+        in_specs=[vmem] * 8,
         out_specs=vmem,
         out_shape=jax.ShapeDtypeStruct((HEADS, TOK, LAT), BF16),
         scratch_shapes=[pltpu.VMEM((TOK, HEADS, LAT), BF16)],
-        compiler_params=params(32),
+        compiler_params=params(30),
         cost_estimate=pl.CostEstimate(
-            flops=2 * samples * rows * (2 * half + SUF) * (width + LAT),
+            flops=2 * samples * rows * (half * width + (2 * half + SUF) * LAT),
             bytes_accessed=8 * 1024 * 1024,
             transcendentals=samples * rows * (2 * half + SUF),
         ),
         name="attend",
-    )(lens, q, ka, kb, own, fresh)
+    )(q, own, *scored, ka, kb, fresh)
 
 
 def project_body(core_ref, x_ref, uva_ref, uvb_ref, oa_ref, ob_ref, out_ref):
@@ -203,7 +279,6 @@
 
 CHUNK = 512
 PIECES = D // CHUNK
-FLYING = 5
 
 
 def expert_body(x, wg, wu, wd_hbm, out_ref, xs, wd, mid, res, sems):
@@ -214,14 +289,8 @@
     for c in range(PIECES):
         span = pl.ds(c * CHUNK, CHUNK)
         loads.append(pltpu.make_async_copy(wd_hbm.at[0, :, span], wd.at[:, span], sems.at[c]))
-    for i in range(FLYING):
-        loads[i].start()
-
-    def take(i):
-        loads[i].wait()
-        if i + FLYING < len(loads):
-            loads[i + FLYING].start()
-
+    for load in loads:
+        load.start()
     n = lines // 4
     out_row, in_row = iota((n, n), 0), iota((n, n), 1)
     perm = (in_row == (out_row % group) * QTR + out_row // group).astype(BF16)
@@ -235,7 +304,7 @@
     up = dot(xs[...], wu[0])
     mid[...] = (gate * up).astype(BF16)
     for c in range(PIECES):
-        take(c)
+        loads[c].wait()
         span = slice(c * CHUNK, (c + 1) * CHUNK)
         res[:, span] = dot(mid[...], wd[:, span]).astype(BF16)
     for i in range(4):
@@ -307,14 +376,13 @@
     samples = query.shape[1]
     n_smp = lax.axis_size("smp")
     chips = n_smp // 2
-    prompts, span, width = prefill_cache.shape[1:]
+    prompts, _, width = prefill_cache.shape[1:]
     core = lax.axis_index("smp") % 2
     pair = [(i, i ^ 1) for i in range(n_smp)]
     same_core = [[2 * k + c for k in range(chips)] for c in range(2)]
 
     shared = n_smp // prompts // 2
-    slab = prefill_cache[0].reshape(prompts, 1, 2, span // 2, width)
-    outgoing = jnp.broadcast_to(slab, (prompts, shared, 2, span // 2, width)).reshape(n_smp, span // 2, width)
+    outgoing = pack(prefill_cache[0], shared).reshape(n_smp, LINES, 128)
     half_a = lax.all_to_all(outgoing, "smp", 0, 0, tiled=True)
 
     half_a, ids, weights, gain = lax.optimization_barrier((half_a, expert_ids, route_weights, ffn_gain))
@@ -322,17 +390,15 @@
     send, mix = route(ids.reshape(TOK, TOP), weights.reshape(TOK, TOP))
     gain = gain.reshape(1, D)
     core = core.reshape(1)
-    half_b, send, mix, gain, core, w_uv, w_out = lax.optimization_barrier(
-        (half_b, send, mix, gain, core, w_uv, w_out)
+    own = jnp.swapaxes(suffix_cache[0], 1, 2)
+    q = query.reshape(samples, STEPS * HEADS, width)
+    scored = score(suffix_len, q, half_a, own, new_latent[0])
+    half_b, scored, send, mix, gain, core, w_uv, w_out = lax.optimization_barrier(
+        (half_b, scored, send, mix, gain, core, w_uv, w_out)
     )
     uv_b = lax.ppermute(w_uv, "smp", pair)
     out_b = lax.ppermute(w_out, "smp", pair)
-    half_a = half_a.reshape(-1, width)
-    half_b = half_b.reshape(-1, width)
-    own = jnp.swapaxes(suffix_cache[0], 1, 2)
-    context = attend(
-        suffix_len, query.reshape(samples, STEPS * HEADS, width), half_a, half_b, own, new_latent[0]
-    )
+    context = attend(q, own, scored, half_a, half_b, new_latent[0])
     context, uv_b, out_b = lax.optimization_barrier((context, uv_b, out_b))
     by_chip = context.reshape(chips, HEADS // chips, TOK, LAT)
     by_heads = lax.all_to_all(by_chip, "smp", 0, 0, tiled=True, axis_index_groups=same_core)

time: 174 us -> 169 us (0.971)
  local copies, waits for them, and re-layouts: 3.75 us -> 1.16 us
  waiting for transfers between devices: 2.44 us -> 0.01 us
    ppermute x1, waiting for transfers between devices: 2.44 us -> 0.01 us  [on_device(): half_b = lax.ppermute(half_a, 'smp', pair)]
    pallas_call x1 -> x3, Pallas kernels: 9.3 us -> 10.1 us  [the longest x1 6.82 us: attend(): pl.pallas_call(attend_body, in_specs=[vmem] * 8, out_specs=vmem, out_shap...]
  transfers between devices with their start and end apart: 3 -> 3, of which waited for: 1 -> 0; matrix products, arithmetic and copies ran while one was open for 0% -> 0% of each run, Pallas kernels for 6% -> 6%
where the time goes in v1:
time: 169 us; the launch traced here: 168 us
  blocking collectives  143 us (85%)
  Pallas kernels  23.4 us (14%)
    all_to_all x1, blocking collectives, on_device(): arrived = lax.all_to_all(rows, ('grp', 'smp'), 0, 0, tiled=True)  36 us
    all_to_all x1, blocking collectives, on_device(): returned = lax.all_to_all(answered, ('grp', 'smp'), 0, 0, tiled=True)  31.8 us
    all_to_all x1, blocking collectives, on_device(): half_a = lax.all_to_all(outgoing, 'smp', 0, 0, tiled=True)  28.5 us
    all_to_all x1, blocking collectives, on_device(): lax.all_to_all(shares, 'smp', 0, 0, tiled=True, axis_index_groups=same_core)  27.7 us
    all_to_all x1, blocking collectives, on_device(): lax.all_to_all(by_chip, 'smp', 0, 0, tiled=True, axis_index_groups=same_c...  18.6 us
    pallas_call x1, Pallas kernels, expert(): pl.pallas_call(expert_body, in_specs=[vmem, vmem, vmem, hbm], out_specs=v...  9.28 us
    pallas_call x1, Pallas kernels, attend(): pl.pallas_call(attend_body, in_specs=[vmem] * 8, out_specs=vmem, out_shap...  6.82 us
  transfers between devices with their start and end apart: 3, of which 0 were waited for; matrix products, arithmetic and copies ran while one was open for 0% of the time, Pallas kernels for 6%

profile of v1, /device:TPU:1, one launch (start us, length us, event | category | flops | bytes accessed | tf_op | source)
XLA Modules:
  0.0 168.4 jit_solution(16105048977757690349)
XLA Ops:
  0.0 0.0 copy-start.1
  0.0 1.1 copy-done.1
  1.1 0.0 copy-start.10
  1.1 0.0 copy-start.4
  1.1 0.0 copy-start.5
  1.1 0.0 copy-start.6
  1.1 0.0 copy-start.7
  1.1 0.0 copy-start.8
  1.1 0.0 copy-start.9
  1.1 0.2 pack.1
  1.3 28.5 %all_to_all.25.ka_ref = bf16[32,144,128]{2,1,0:T(8,128)(2,1)S(1)} all-to-all(bf16[32,144,128]{2,1,0:T(8,128)(2,1)S(1)} %bitcast.23), channel_id=1, replica_groups=mesh['grp'=4,'smp'=32] {'smp'}, dimensions={0} | all-to-all | bytes 2359296 | tf_op jit(solution)/shard_map/all_to_all | solution.py:386
  29.8 0.4 collective-permute-start
  30.2 0.0 copy-done.10
  30.2 0.0 copy-done.4
  30.2 0.0 copy-done.5
  30.2 0.5 route.1
  30.7 0.0 copy-done.6
  30.7 0.0 copy-done.7
  30.7 0.0 copy-done.8
  30.7 0.0 copy-done.9
  30.7 0.0 copy-start
  30.8 0.0 copy-start.2
  30.8 3.1 %score.1 = (f32[4,256,1024]{2,1,0:T(8,128)S(1)}, f32[4,256,128]{2,1,0:T(8,128)S(1)}, f32[4,256,4]{2,1,0:T(8,128)S(1)}) custom-call(s32[1,4]{1,0:T(1,128)S(1)} %copy-done.9, bf16[4,256,576]{2,1,0:T(8,128)(2,1)S(1)} %bitcast.30, bf16[32,144,128]{2,1,0:T(8,128)(2,1)S(1)} %all_to_all.25.ka_ref, bf16[4,576,128]{2,1,0:T(8,128)(2,1)S(1)} %bitcast.32, ...), custom_call_target="tpu_custom_call" | custom-call | flops 1358954496 | bytes 2097152 | tf_op jit(solution)/shard_map/score/pallas_call | solution.py:108
  33.9 0.0 collective-permute-done.kb_ref
  33.9 0.0 copy-done
  33.9 0.2 collective-permute-start.2
  34.1 0.0 copy-done.2
  34.1 0.4 collective-permute-start.1
  34.5 0.0 slice-start.2
  34.5 6.8 %attend.1 = bf16[64,16,512]{2,1,0:T(8,128)(2,1)S(1)} custom-call(bf16[4,256,576]{2,1,0:T(8,128)(2,1)S(1)} %bitcast.31, bf16[4,576,128]{2,1,0:T(8,128)(2,1)S(1)} %bitcast.33, f32[4,256,1024]{2,1,0:T(8,128)S(1)} %get-tuple-element.40.sa_ref, f32[4,256,128]{2,1,0:T(8,128)S(1)} %get-tuple-element.41.so_ref, f32[4,256,4]{2,1,0:T(8,128)S(1)} %get-tuple-element.42.sf_ref, ...), custom_call_target="tpu_custom_call" | custom-call | flops 3489660928 | bytes 8388608 | tf_op jit(solution)/shard_map/attend/pallas_call | solution.py:166
  41.3 0.0 collective-permute-done.1.uvb_ref
  41.3 0.0 collective-permute-done.2.ob_ref
  41.4 18.6 %all_to_all.26.x_ref = bf16[16,4,16,512]{3,2,1,0:T(8,128)(2,1)S(1)} all-to-all(bf16[16,4,16,512]{3,2,1,0:T(8,128)(2,1)S(1)} %bitcast.25), channel_id=1, replica_groups={{0,2,4,6,8,10,12,14,16,18,20,22,24,26,28,30},{1,3,5,7,9,11,13,15,17,19,..., dimensions={0} | all-to-all | bytes 2097152 | tf_op jit(solution)/shard_map/all_to_all | solution.py:404
  60.0 0.0 slice-start
  60.0 1.4 project.1
  61.4 0.0 copy-start.3
  61.4 0.0 slice-start.1
  61.4 27.7 %all_to_all.27.parts_ref = bf16[16,16,3584]{2,1,0:T(8,128)(2,1)S(1)} all-to-all(bf16[16,16,3584]{2,1,0:T(8,128)(2,1)S(1)} %project.1), channel_id=1, replica_groups={{0,2,4,6,8,10,12,14,16,18,20,22,24,26,28,30},{1,3,5,7,9,11,13,15,17,19,..., dimensions={0} | all-to-all | bytes 3670016 | tf_op jit(solution)/shard_map/all_to_all | solution.py:406
  89.2 0.0 copy-done.3
  89.2 1.0 dispatch.1
  90.2 36.0 %all_to_all.28 = bf16[128,8,896]{2,1,0:T(8,128)(2,1)S(1)} all-to-all(bf16[128,8,896]{2,1,0:T(8,128)(2,1)S(1)} %bitcast.24), channel_id=1, replica_groups=mesh['grp'=4,'smp'=32] {'grp','smp'}, dimensions={0} | all-to-all | bytes 3670016 | tf_op jit(solution)/shard_map/all_to_all | solution.py:410
  126.2 0.0 slice-done.2
  126.2 0.0 slice-done
  126.2 0.0 slice-done.3
  126.2 0.0 slice-done.1
  126.2 9.3 %expert.1 = bf16[1024,896]{1,0:T(8,128)(2,1)S(1)} custom-call(bf16[1024,896]{1,0:T(8,128)(2,1)S(1)} %bitcast.16, bf16[1,3584,1024]{2,1,0:T(8,128)(2,1)S(1)} %bitcast.20, bf16[1,3584,1024]{2,1,0:T(8,128)(2,1)S(1)} %bitcast.22, bf16[1,1024,3584]{2,1,0:T(8,128)(2,1)} %wd_hbm.1), custom_call_target="tpu_custom_call" | custom-call | flops 5637144576 | bytes 27262976 | tf_op jit(solution)/shard_map/expert/pallas_call | solution.py:320
  135.5 31.8 %all_to_all.29 = bf16[128,8,896]{2,1,0:T(8,128)(2,1)S(1)} all-to-all(bf16[128,8,896]{2,1,0:T(8,128)(2,1)S(1)} %bitcast.17), channel_id=1, replica_groups=mesh['grp'=4,'smp'=32] {'grp','smp'}, dimensions={0} | all-to-all | bytes 3670016 | tf_op jit(solution)/shard_map/all_to_all | solution.py:413
  167.3 1.1 combine.1
  (4 shorter events, 0.0 us)
Async XLA Ops:
  0.0 1.1 copy-start.1
  1.1 29.1 %copy-start.10 = (bf16[3584]{0:T(1024)(128)(2,1)S(1)}, bf16[3584]{0:T(1024)(128)(2,1)}, u32[]{:S(2)}) copy-start(bf16[3584]{0:T(1024)(128)(2,1)} %param.22) | copy-start | bytes 21508
  1.1 29.1 %copy-start.4 = (s32[1,4,4,8]{3,2,1,0:T(4,128)S(1)}, s32[1,4,4,8]{3,2,1,0:T(4,128)}, u32[]{:S(2)}) copy-start(s32[1,4,4,8]{3,2,1,0:T(4,128)} %param.23) | copy-start | bytes 1540
  1.1 29.1 %copy-start.5 = (f32[1,4,4,8]{3,2,1,0:T(4,128)S(1)}, f32[1,4,4,8]{3,2,1,0:T(4,128)}, u32[]{:S(2)}) copy-start(f32[1,4,4,8]{3,2,1,0:T(4,128)} %param.24) | copy-start | bytes 1540
  1.1 29.6 %copy-start.6 = (bf16[1,4,4,64,576]{4,3,2,1,0:T(8,128)(2,1)S(1)}, bf16[1,4,4,64,576]{4,3,2,1,0:T(8,128)(2,1)}, u32[]{:S(2)}) copy-start(bf16[1,4,4,64,576]{4,3,2,1,0:T(8,128)(2,1)} %param.15) | copy-start | bytes 3538948
  1.1 29.6 %copy-start.7 = (bf16[1,4,128,576]{2,3,1,0:T(8,128)(2,1)S(1)}, bf16[1,4,128,576]{2,3,1,0:T(8,128)(2,1)}, u32[]{:S(2)}) copy-start(bf16[1,4,128,576]{2,3,1,0:T(8,128)(2,1)} %param.17) | copy-start | bytes 1769476
  1.1 29.6 %copy-start.8 = (bf16[1,4,4,576]{3,2,1,0:T(4,128)(2,1)S(1)}, bf16[1,4,4,576]{3,2,1,0:T(4,128)(2,1)}, u32[]{:S(2)}) copy-start(bf16[1,4,4,576]{3,2,1,0:T(4,128)(2,1)} %param.19) | copy-start | bytes 55300
  1.1 29.6 %copy-start.9 = (s32[1,4]{1,0:T(1,128)S(1)}, s32[1,4]{1,0:T(1,128)}, u32[]{:S(2)}) copy-start(s32[1,4]{1,0:T(1,128)} %len_ref.1) | copy-start | bytes 52
  29.8 4.1 %collective-permute-start = (bf16[32,144,128]{2,1,0:T(8,128)(2,1)S(1)}, bf16[32,144,128]{2,1,0:T(8,128)(2,1)}, u32[]{:S(2)}, u32[]{:S(2)}) collective-permute-start(bf16[32,144,128]{2,1,0:T(8,128)(2,1)S(1)} %all_to_all.25.ka_ref), channel_id=1, source_target_pairs={{0,1},{1,0},{2,3},{3,2},{4,5},{5,4},{6,7},{7,6},{8,9},{9,8},{10,11... | collective-permute-start | bytes 3538952 | tf_op jit(solution)/shard_map/ppermute | solution.py:389
  30.7 3.2 %copy-start = (bf16[2,128,3584]{2,1,0:T(8,128)(2,1)S(1)}, bf16[2,128,3584]{2,1,0:T(8,128)(2,1)}, u32[]{:S(2)}) copy-start(bf16[2,128,3584]{2,1,0:T(8,128)(2,1)} %oa_ref) | copy-start | bytes 5505028
  30.8 3.4 %copy-start.2 = (bf16[2,512,128]{2,1,0:T(8,128)(2,1)S(1)}, bf16[2,512,128]{2,1,0:T(8,128)(2,1)}, u32[]{:S(2)}) copy-start(bf16[2,512,128]{2,1,0:T(8,128)(2,1)} %uva_ref) | copy-start | bytes 786436
  33.9 7.4 %collective-permute-start.2 = (bf16[2,128,3584]{2,1,0:T(8,128)(2,1)S(1)}, bf16[2,128,3584]{2,1,0:T(8,128)(2,1)S(1)}, u32[]{:S(2)}, u32[]{:S(2)}) collective-permute-start(bf16[2,128,3584]{2,1,0:T(8,128)(2,1)S(1)} %copy-done), channel_id=1, source_target_pairs={{0,1},{1,0},{2,3},{3,2},{4,5},{5,4},{6,7},{7,6},{8,9},{9,8},{10,11... | collective-permute-start | bytes 5505032 | tf_op jit(solution)/shard_map/ppermute | solution.py:400
  34.1 7.2 %collective-permute-start.1 = (bf16[2,512,128]{2,1,0:T(8,128)(2,1)S(1)}, bf16[2,512,128]{2,1,0:T(8,128)(2,1)S(1)}, u32[]{:S(2)}, u32[]{:S(2)}) collective-permute-start(bf16[2,512,128]{2,1,0:T(8,128)(2,1)S(1)} %copy-done.2), channel_id=1, source_target_pairs={{0,1},{1,0},{2,3},{3,2},{4,5},{5,4},{6,7},{7,6},{8,9},{9,8},{10,11... | collective-permute-start | bytes 786440 | tf_op jit(solution)/shard_map/ppermute | solution.py:399
  34.5 91.7 %slice-start.2 = ((s8[7340032]{0:T(1024)(128)(4,1)}), s8[4194304]{0:T(1024)(128)(4,1)S(1)}, s32[]{:S(2)}) async-start(s8[7340032]{0:T(1024)(128)(4,1)} %bitcast.21), calls=%async_computation.7 | async-start | bytes 8388608
  60.0 66.2 %slice-start = ((s8[7340032]{0:T(1024)(128)(4,1)}), s8[4194304]{0:T(1024)(128)(4,1)S(1)}, s32[]{:S(2)}) async-start(s8[7340032]{0:T(1024)(128)(4,1)} %bitcast.19), calls=%async_computation.5 | async-start | bytes 8388608
  60.0 66.2 %slice-start.3 = ((s8[7340032]{0:T(1024)(128)(4,1)}), s8[3145728]{0:T(1024)(128)(4,1)S(1)}, s32[]{:S(2)}) async-start(s8[7340032]{0:T(1024)(128)(4,1)} %bitcast.21), calls=%async_computation.8 | async-start | bytes 6291456
  61.4 27.8 %copy-start.3 = (bf16[1,4,4,3584]{3,2,1,0:T(4,128)(2,1)S(1)}, bf16[1,4,4,3584]{3,2,1,0:T(4,128)(2,1)}, u32[]{:S(2)}) copy-start(bf16[1,4,4,3584]{3,2,1,0:T(4,128)(2,1)} %param.14) | copy-start | bytes 344068
  61.4 64.8 %slice-start.1 = ((s8[7340032]{0:T(1024)(128)(4,1)}), s8[3145728]{0:T(1024)(128)(4,1)S(1)}, s32[]{:S(2)}) async-start(s8[7340032]{0:T(1024)(128)(4,1)} %bitcast.19), calls=%async_computation.6 | async-start | bytes 6291456
